TPU v7x, 32 devices: a whole 2x2x4 slice. The times are simulated.
32 devices in a mesh: expert: 8 (over y, x, core), pair: 4 (over z).
Axes of the slice: x: 2, y: 2, z: 4, core: 2. Of those that a mesh axis runs over, the one named last changes fastest.
Arguments:
- tokens: bfloat16 [4096, 4096], P(('expert', 'pair')), may hold values from -6 to 6
- expert_ids: int32 [4096, 8], P(('expert', 'pair')), may hold values from 0 to 127, all different within a row
- route_weight: float32 [4096, 8], P(('expert', 'pair')), may hold values from 0.1 to 1
- gate_weight: bfloat16 [8, 4096, 768], P('expert'), may hold values from -0.09375 to 0.09375
- up_weight: bfloat16 [8, 4096, 768], P('expert'), may hold values from -0.09375 to 0.09375
- down_weight: bfloat16 [8, 768, 4096], P('expert'), may hold values from -0.21875 to 0.21875
Outputs:
- combined: bfloat16 [4096, 4096], P(('expert', 'pair'))
- hessian: float32 [8, 768, 768], P('expert', 'pair')
- panel: float32 [8, 768, 128], P('expert', 'pair')
Inputs may be any that keep to these rules, and one draw needn't show every extreme that they name: `expert_ids`: each row names 8 different experts, and every expert is named by some row.
All inputs are finite; a program needn't handle non-finite values.
Results may differ from a plain program's by a relative error of at most 0.0057.
Values may be sent and summed in bfloat16 or wider, within the bound.
A program may use at most 128 MiB of HBM per device.

v0:
```python
import jax
import jax.numpy as jnp
from jax import lax
from jax.sharding import PartitionSpec as P

EXPERTS = 128
FF = 768
PANEL = 128
CAP = 16


def swiglu_rows(flat_rows, gate_matrix, upper_matrix, down_matrix):
    gate_value = jnp.dot(flat_rows, gate_matrix, preferred_element_type=jnp.float32)
    upper_value = jnp.dot(flat_rows, upper_matrix, preferred_element_type=jnp.float32)
    hidden = (jax.nn.silu(gate_value) * upper_value).astype(jnp.bfloat16)
    output = jnp.dot(hidden, down_matrix, preferred_element_type=jnp.float32).astype(jnp.bfloat16)
    return (hidden, output)


def per_device(tokens, expert_ids, route_weight, gate_weight, up_weight, down_weight):
    owners = lax.axis_size("expert")
    pair_count = lax.axis_size("pair")
    tok_count = tokens.shape[0]
    model_width = tokens.shape[1]
    per_owner = EXPERTS // owners
    in_flight = expert_ids % per_owner == 0
    owner_of = expert_ids // per_owner
    columns = lax.broadcasted_iota(jnp.int32, (1, 1, owners), 2)
    route_hit = (in_flight[:, :, None] & (owner_of[:, :, None] == columns)).astype(jnp.int32)
    picked = jnp.sum(route_hit, axis=1)
    before = jnp.cumsum(picked, axis=0) - picked
    kept_rows = picked * (before < CAP).astype(jnp.int32)
    slot_ids = lax.broadcasted_iota(jnp.int32, (1, 1, CAP), 2)
    slot_marks = kept_rows[:, :, None] * (before[:, :, None] == slot_ids).astype(jnp.int32)
    token_number = lax.broadcasted_iota(jnp.int32, (tok_count, 1, 1), 0) + 1
    source_row = jnp.sum(slot_marks * token_number, axis=0) - 1
    source_flat = source_row.reshape(-1)
    picked_rows = jnp.take(tokens, jnp.maximum(source_flat, 0), axis=0)
    outgoing = jnp.where((source_flat >= 0)[:, None], picked_rows, jnp.zeros_like(picked_rows))
    outgoing = outgoing.reshape(owners, CAP, model_width)
    gate_matrix = gate_weight[0]
    upper_matrix = up_weight[0]
    down_matrix = down_weight[0]
    arrived = lax.all_to_all(outgoing, "expert", split_axis=0, concat_axis=0, tiled=True)
    item_count = arrived.shape[1]
    hidden, output = swiglu_rows(
        arrived.reshape(-1, model_width), gate_matrix, upper_matrix, down_matrix
    )
    hidden_slots = hidden.reshape(owners, item_count, -1)
    results = output.reshape(owners, item_count, model_width)
    hidden_rows = hidden_slots.reshape(-1, hidden_slots.shape[2])
    returned = lax.all_to_all(results, "expert", split_axis=0, concat_axis=0, tiled=True)
    returned_flat = returned.reshape(-1, model_width)
    rank_choice = jnp.sum(route_hit * before[:, None, :], axis=2)
    keep_choice = jnp.sum(route_hit * kept_rows[:, None, :], axis=2)
    slot_index = jnp.minimum(owner_of, owners - 1) * CAP + jnp.minimum(rank_choice, CAP - 1)
    weights = route_weight * keep_choice.astype(jnp.float32)
    combined = jnp.zeros((tok_count, model_width), jnp.float32)
    for column_index in range(expert_ids.shape[1]):
        fetched = jnp.take(returned_flat, slot_index[:, column_index], axis=0)
        combined = combined + weights[:, column_index : column_index + 1] * fetched.astype(
            jnp.float32
        )
    hess_scale = 2.0 / (CAP * owners * pair_count)
    local_sum = (
        lax.dot_general(
            hidden_rows, hidden_rows, (((0,), (0,)), ((), ())), preferred_element_type=jnp.float32
        )
        * hess_scale
    )
    row_share = FF // pair_count
    pair_place = lax.axis_index("pair")
    whole_sum = lax.psum(local_sum, "pair")
    damping = 0.01 * jnp.trace(whole_sum) / FF
    corner = whole_sum[:PANEL, :PANEL]
    my_rows = lax.dynamic_slice_in_dim(whole_sum, pair_place * row_share, row_share, 0)
    lower_factor = jnp.linalg.cholesky(corner + damping * jnp.eye(PANEL, dtype=jnp.float32))
    row_ids = pair_place * row_share + lax.broadcasted_iota(jnp.int32, (row_share, PANEL), 0)
    column_ids = lax.broadcasted_iota(jnp.int32, (row_share, PANEL), 1)
    leading = my_rows[:, :PANEL] + damping * (row_ids == column_ids).astype(jnp.float32)
    panel_rows = jax.scipy.linalg.solve_triangular(lower_factor, leading.T, lower=True).T
    return (combined.astype(jnp.bfloat16), my_rows[None], panel_rows[None])


def solution(mesh):
    in_specs = (
        P(("expert", "pair"), None),
        P(("expert", "pair"), None),
        P(("expert", "pair"), None),
        P("expert", None, None),
        P("expert", None, None),
        P("expert", None, None),
    )
    out_specs = (P(("expert", "pair"), None), P("expert", "pair", None), P("expert", "pair", None))
    return jax.shard_map(
        per_device, mesh=mesh, in_specs=in_specs, out_specs=out_specs, check_vma=False
    )
```

profile of v0, /device:TPU:0, one launch (start us, length us, event | category | flops | bytes accessed | tf_op | source)
XLA Modules:
  0.0 176.9 jit_solution(13057356022462531856)
XLA Ops:
  7.2 0.0 copy-start
  7.2 0.9 copy.19
  8.2 0.1 copy.22
  8.3 0.1 copy.25
  8.4 0.2 reduce_window_sum.11
  8.7 0.1 copy.29
  8.7 0.2 multiply_reduce_fusion
  9.0 0.1 max.7
  9.1 0.1 ge.18
  9.2 0.0 copy-done
  9.2 2.2 %gather_fusion = bf16[128,4096]{1,0:T(8,128)(2,1)} fusion(bf16[128,4096]{1,0:T(8,128)(2,1)S(1)} %copy-done, s32[1024]{0:T(1024)S(1)} %pad_clamp_fusion.8), kind=kCustom, calls=%fused_computation.clone | custom fusion | bytes 2097664 | tf_op jit(solution)/shard_map/jit(_take)/gather | solution.py:38
  11.4 2.6 %select_select_fusion = bf16[128,4096]{1,0:T(8,128)(2,1)} fusion(bf16[128,4096]{1,0:T(8,128)(2,1)} %gather_fusion, pred[128]{0:T(512)(128)(4,1)S(1)} %compare_and_fusion.8, pred[128]{0:T(512)(128)(4,1)S(1)} %ge.18), kind=kLoop, calls=%fused_computation.23 | loop fusion | flops 1048576 | bytes 2097408 | tf_op jit(solution)/shard_map/jit(_where)/select_n | solution.py:39
  13.9 5.2 %all-to-all-start = ((bf16[8,16,4096]{2,1,0:T(8,128)(2,1)}), bf16[8,16,4096]{2,1,0:T(8,128)(2,1)}, u32[]{:S(2)}, u32[]{:S(2)}) async-start(bf16[8,16,4096]{2,1,0:T(8,128)(2,1)} %bitcast.63), calls=%async_computation | async-start | bytes 2097152 | tf_op jit(solution)/shard_map/all_to_all | solution.py:44
  19.1 0.0 all-reduce.2.cloned.1.call-start
  19.2 0.1 copy.30
  19.3 0.1 minimum_add_fusion
  19.3 0.4 slice_reduce_fusion.7
  19.9 14.7 %all-to-all-done = bf16[8,16,4096]{2,1,0:T(8,128)(2,1)} async-done(((bf16[8,16,4096]{2,1,0:T(8,128)(2,1)}), bf16[8,16,4096]{2,1,0:T(8,128)(2,1)}, u32[]{:S(2)}, u32[]{:S(2)}) %all-to-all-start) | async-done | bytes 1048608 | tf_op jit(solution)/shard_map/all_to_all | solution.py:44
  34.6 4.2 %fusion.4 = f32[128,768]{1,0:T(8,128)S(1)} fusion(bf16[128,4096]{1,0:T(8,128)(2,1)} %bitcast.2, bf16[1,4096,768]{2,1,0:T(8,128)(2,1)} %param.11), kind=kOutput, calls=%fused_computation.13 | convolution fusion | flops 805306368 | bytes 7733248 | tf_op jit(solution)/shard_map/dot_general | solution.py:13
  38.9 0.0 slice-done
  38.9 0.0 slice-done.1
  38.9 2.2 %fusion.12 = bf16[128,768]{1,0:T(8,128)(2,1)S(1)} fusion(bf16[128,4096]{1,0:T(8,128)(2,1)} %bitcast.2, bf16[1,4096,768]{2,1,0:T(8,128)(2,1)S(1)} %bitcast.62, f32[128,768]{1,0:T(8,128)S(1)} %fusion.4), kind=kOutput, calls=%fused_computation.21 | convolution fusion | flops 805896192 | bytes 7929856 | tf_op jit(solution)/shard_map/dot_general | solution.py:14
  41.1 1.9 %convolution_multiply_fusion = f32[768,768]{1,0:T(8,128)} fusion(bf16[128,768]{1,0:T(8,128)(2,1)S(1)} %fusion.12), kind=kOutput, calls=%fused_computation.19 | convolution fusion | flops 151584768 | bytes 2555904 | tf_op jit(solution)/shard_map/dot_general | solution.py:66
  43.0 0.0 all-reduce.2.cloned.1.call-update
  43.1 4.8 %fusion.6 = bf16[128,4096]{1,0:T(8,128)(2,1)} fusion(bf16[128,768]{1,0:T(8,128)(2,1)S(1)} %fusion.12, bf16[1,768,4096]{2,1,0:T(8,128)(2,1)} %param.13), kind=kOutput, calls=%fused_computation.15 | convolution fusion | flops 805830656 | bytes 7536640 | tf_op jit(solution)/shard_map/dot_general | solution.py:16
  47.8 3.9 %all-to-all-start.1 = ((bf16[8,16,4096]{2,1,0:T(8,128)(2,1)}), bf16[8,16,4096]{2,1,0:T(8,128)(2,1)S(1)}, u32[]{:S(2)}, u32[]{:S(2)}) async-start(bf16[8,16,4096]{2,1,0:T(8,128)(2,1)} %bitcast.6), calls=%async_computation.1 | async-start | bytes 2097152 | tf_op jit(solution)/shard_map/all_to_all | solution.py:52
  51.7 0.0 copy-done.1
  51.8 15.1 %all-to-all-done.1 = bf16[8,16,4096]{2,1,0:T(8,128)(2,1)S(1)} async-done(((bf16[8,16,4096]{2,1,0:T(8,128)(2,1)}), bf16[8,16,4096]{2,1,0:T(8,128)(2,1)S(1)}, u32[]{:S(2)}, u32[]{:S(2)}) %all-to-all-start.1) | async-done | bytes 1048608 | tf_op jit(solution)/shard_map/all_to_all | solution.py:52
  66.8 1.2 gather_fusion.8
  68.0 2.2 %gather_fusion.7 = bf16[128,4096]{1,0:T(8,128)(2,1)} fusion(bf16[128,4096]{1,0:T(8,128)(2,1)S(1)} %bitcast.54, s32[1024]{0:T(1024)S(1)} %pad_clamp_fusion.1), kind=kCustom, calls=%fused_computation.7.clone | custom fusion | bytes 2097664 | tf_op jit(solution)/shard_map/jit(_take)/gather | solution.py:60
  70.2 2.2 %gather_fusion.6 = bf16[128,4096]{1,0:T(8,128)(2,1)} fusion(bf16[128,4096]{1,0:T(8,128)(2,1)S(1)} %bitcast.55, s32[1024]{0:T(1024)S(1)} %pad_clamp_fusion.2), kind=kCustom, calls=%fused_computation.6.clone | custom fusion | bytes 2097664 | tf_op jit(solution)/shard_map/jit(_take)/gather | solution.py:60
  72.4 2.2 %gather_fusion.5 = bf16[128,4096]{1,0:T(8,128)(2,1)} fusion(bf16[128,4096]{1,0:T(8,128)(2,1)S(1)} %bitcast.56, s32[1024]{0:T(1024)S(1)} %pad_clamp_fusion.3), kind=kCustom, calls=%fused_computation.5.clone | custom fusion | bytes 2097664 | tf_op jit(solution)/shard_map/jit(_take)/gather | solution.py:60
  74.6 2.2 %gather_fusion.4 = bf16[128,4096]{1,0:T(8,128)(2,1)} fusion(bf16[128,4096]{1,0:T(8,128)(2,1)S(1)} %bitcast.57, s32[1024]{0:T(1024)S(1)} %pad_clamp_fusion.4), kind=kCustom, calls=%fused_computation.4.clone | custom fusion | bytes 2097664 | tf_op jit(solution)/shard_map/jit(_take)/gather | solution.py:60
  76.8 2.3 %gather_fusion.3 = bf16[128,4096]{1,0:T(8,128)(2,1)} fusion(bf16[128,4096]{1,0:T(8,128)(2,1)S(1)} %bitcast.58, s32[1024]{0:T(1024)S(1)} %pad_clamp_fusion.5), kind=kCustom, calls=%fused_computation.3.clone | custom fusion | bytes 2097664 | tf_op jit(solution)/shard_map/jit(_take)/gather | solution.py:60
  79.0 2.2 %gather_fusion.2 = bf16[128,4096]{1,0:T(8,128)(2,1)} fusion(bf16[128,4096]{1,0:T(8,128)(2,1)S(1)} %bitcast.59, s32[1024]{0:T(1024)S(1)} %pad_clamp_fusion.6), kind=kCustom, calls=%fused_computation.2.clone | custom fusion | bytes 2097664 | tf_op jit(solution)/shard_map/jit(_take)/gather | solution.py:60
  81.3 2.2 %gather_fusion.1 = bf16[128,4096]{1,0:T(8,128)(2,1)} fusion(bf16[128,4096]{1,0:T(8,128)(2,1)S(1)} %bitcast.60, s32[1024]{0:T(1024)S(1)} %pad_clamp_fusion.7), kind=kCustom, calls=%fused_computation.1.clone | custom fusion | bytes 2097664 | tf_op jit(solution)/shard_map/jit(_take)/gather | solution.py:60
  83.5 6.2 %add_convert_fusion = bf16[128,4096]{1,0:T(8,128)(2,1)} fusion(bf16[128,4096]{1,0:T(8,128)(2,1)S(1)} %gather_fusion.8, bf16[128,4096]{1,0:T(8,128)(2,1)} %gather_fusion.7, bf16[128,4096]{1,0:T(8,128)(2,1)} %gather_fusion.6, bf16[128,4096]{1,0:T(8,128)(2,1)} %gather_fusion.5, bf16[128,4096]{1,0:T(8,128)(2,1)} %gather_fusion.4, ...), kind=kLoop, calls=%fused_computation.18 | loop fusion | flops 16777216 | bytes 9442304 | tf_op jit(solution)/shard_map/convert_element_type | solution.py:82
  89.6 49.0 %all-reduce.2.cloned.1.call-done = f32[768,768]{1,0:T(8,128)} async-done(((f32[768,768]{1,0:T(8,128)}), f32[768,768]{1,0:T(8,128)}) %all-reduce.2.cloned.1.call-update) | async-done | bytes 2359312 | tf_op jit(solution)/shard_map/psum | solution.py:73
  138.6 2.4 %select_reduce_fusion = f32[]{:T(128)} fusion(f32[768,768]{1,0:T(8,128)} %all-reduce.2.cloned.1.call-done), kind=kLoop, calls=%fused_computation.16 | loop fusion | flops 1769471 | bytes 2359300 | tf_op jit(solution)/shard_map/jit(trace)/reduce_sum | solution.py:74
  141.7 0.9 slice_add_fusion
  142.5 0.1 copy.33
  142.6 0.9 fusion.19
  143.5 11.7 %cholesky.16 = f32[128,128]{1,0:T(8,128)S(1)} custom-call(f32[128,128]{1,0:T(8,128)S(1)} %fusion.19), custom_call_target="Cholesky" | custom-call | tf_op jit(solution)/shard_map/jit(cholesky)/cholesky | solution.py:77
  155.2 0.6 compare_reduce_fusion
  155.9 0.7 fusion.16
  156.5 9.8 %custom-call.7 = f32[1,128,128]{1,2,0:T(8,128)S(1)} custom-call(f32[1,128,128]{2,1,0:T(8,128)S(1)} %fusion.16), custom_call_target="InvertDiagBlocksLowerTriangular" | custom-call | tf_op jit(solution)/shard_map/jit(_solve_triangular)/triangular_solve | solution.py:81
  166.4 1.9 %dynamic-slice_bitcast_fusion = f32[1,192,768]{2,1,0:T(8,128)} fusion(f32[768,768]{1,0:T(8,128)} %all-reduce.2.cloned.1.call-done, s32[]{:T(128)S(6)} %select_n.38), kind=kLoop, calls=%fused_computation.24 | loop fusion | bytes 1179652 | tf_op jit(solution)/shard_map/broadcast_in_dim | solution.py:82
  168.3 1.8 %convolution_bitcast_fusion = f32[1,192,128]{2,1,0:T(8,128)} fusion(f32[768,768]{1,0:T(8,128)} %all-reduce.2.cloned.1.call-done, s32[]{:T(128)S(6)} %select_n.38, f32[1,128,128]{1,2,0:T(8,128)S(1)} %custom-call.7, f32[]{:T(128)S(6)} %div.32, s32[192]{0:T(256)S(1)} %iota_add_fusion), kind=kOutput, calls=%fused_computation.22 | convolution fusion | flops 37822464 | bytes 262920 | tf_op jit(solution)/shard_map/jit(_solve_triangular)/triangular_solve | solution.py:81
  (37 shorter events, 0.4 us)
Async XLA Ops:
  7.2 2.0 %copy-start = (bf16[128,4096]{1,0:T(8,128)(2,1)S(1)}, bf16[128,4096]{1,0:T(8,128)(2,1)}, u32[]{:S(2)}) copy-start(bf16[128,4096]{1,0:T(8,128)(2,1)} %param.8) | copy-start | bytes 3145732
  11.4 27.5 %slice-start = ((s8[6291456]{0:T(1024)(128)(4,1)}), s8[2097152]{0:T(1024)(128)(4,1)S(1)}, s32[]{:S(2)}) async-start(s8[6291456]{0:T(1024)(128)(4,1)} %bitcast.61), calls=%async_computation.3 | async-start | bytes 4194304
  13.9 20.7 %all-to-all-start = ((bf16[8,16,4096]{2,1,0:T(8,128)(2,1)}), bf16[8,16,4096]{2,1,0:T(8,128)(2,1)}, u32[]{:S(2)}, u32[]{:S(2)}) async-start(bf16[8,16,4096]{2,1,0:T(8,128)(2,1)} %bitcast.63), calls=%async_computation | async-start | bytes 2097152 | tf_op jit(solution)/shard_map/all_to_all | solution.py:44
  19.1 119.5 %all-reduce.2.cloned.1.call-start = ((), (), s32[]{:S(2)}) async-start(), calls=%async_computation.2 | async-start | bytes 4718592 | tf_op jit(solution)/shard_map/psum | solution.py:73
  34.6 4.3 %slice-start.1 = ((s8[6291456]{0:T(1024)(128)(4,1)}), s8[4194304]{0:T(1024)(128)(4,1)S(1)}, s32[]{:S(2)}) async-start(s8[6291456]{0:T(1024)(128)(4,1)} %bitcast.61), calls=%async_computation.4 | async-start | bytes 8388608
  47.8 3.9 %copy-start.1 = (f32[128,8]{0,1:T(8,128)S(1)}, f32[128,8]{0,1:T(8,128)}, u32[]{:S(2)}) copy-start(f32[128,8]{0,1:T(8,128)} %param.10) | copy-start | bytes 12292
  47.8 19.0 %all-to-all-start.1 = ((bf16[8,16,4096]{2,1,0:T(8,128)(2,1)}), bf16[8,16,4096]{2,1,0:T(8,128)(2,1)S(1)}, u32[]{:S(2)}, u32[]{:S(2)}) async-start(bf16[8,16,4096]{2,1,0:T(8,128)(2,1)} %bitcast.6), calls=%async_computation.1 | async-start | bytes 2097152 | tf_op jit(solution)/shard_map/all_to_all | solution.py:52
Sparse Core Ops, SparseCore 0:
  43.2 95.4 all-reduce.1
where the time goes:
time: 178 us; the launch traced here: 177 us
  waiting for transfers between devices  78.8 us (44%)
  other arithmetic  36.4 us (20%)
  local copies, waits for them, and re-layouts  22.7 us (13%)
  between operations  15 us (8%)
  matrix products  14.9 us (8%)
  starting transfers between devices  9.08 us (5%)
    psum x1, waiting for transfers between devices, per_device(): whole_sum = lax.psum(local_sum, 'pair')  49 us
    gather x8, local copies, waits for them, and re-layouts, per_device(): fetched = jnp.take(returned_flat, slot_index[:, column_index], axis=0)  16.6 us
    all_to_all x1, waiting for transfers between devices, per_device(): lax.all_to_all(results, 'expert', split_axis=0, concat_axis=0, tiled=True)  15.1 us
    all_to_all x1, waiting for transfers between devices, per_device(): lax.all_to_all(outgoing, 'expert', split_axis=0, concat_axis=0, tiled=True)  14.7 us
    another operation x3, other arithmetic, per_device(): jnp.linalg.cholesky(corner + damping * jnp.eye(PANEL, dtype=jnp.float32))  12.4 us
    another operation x2, other arithmetic, per_device(): jax.scipy.linalg.solve_triangular(lower_factor, leading.T, lower=True)  10.5 us
    convert_element_type x1, other arithmetic, per_device(): return (combined.astype(jnp.bfloat16), my_rows[None], panel_rows[None])  6.17 us
    all_to_all x1, starting transfers between devices, per_device(): lax.all_to_all(outgoing, 'expert', split_axis=0, concat_axis=0, tiled=True)  5.17 us
  transfers between devices with their start and end apart: 3, of which 3 were waited for; matrix products, arithmetic and copies ran while one was open for 16% of the time, Pallas kernels for 0%

commit v1 on v0

v1 whole, which is shorter than its diff:
```python
import functools

import jax
import jax.numpy as jnp
from jax import lax
from jax.experimental import pallas as pl
from jax.experimental.pallas import tpu as pltpu
from jax.sharding import PartitionSpec as P

EXPERTS = 128
FF = 768
PANEL = 128
CAP = 16
CHUNKS = 4
MESH = pl.DeviceIdType.MESH
HIGHEST = lax.Precision.HIGHEST


def window_of(place, share):
    start = (place * share) // 128 * 128
    return start, place * share - start


def kernel(
    owners,
    pair_count,
    window,
    tokens_ref,
    ids_ref,
    weight_ref,
    gate_hbm,
    up_hbm,
    down_hbm,
    combined_hbm,
    hessian_hbm,
    panel_hbm,
    gate_buf,
    up_buf,
    down_buf,
    outgoing,
    arrived,
    results,
    returned,
    mixed,
    gate_acc,
    up_acc,
    hidden_all,
    squares,
    elim,
    hess_buf,
    panel_buf,
    load_sem,
    there_send,
    there_recv,
    back_send,
    back_recv,
    pair_send,
    pair_recv,
    store_sem,
):
    me = lax.axis_index("expert")
    place = lax.axis_index("pair")
    tok_count, model_width = tokens_ref.shape
    width = model_width // CHUNKS
    slots = owners * CAP
    per_owner = EXPERTS // owners
    share = FF // pair_count
    hess_scale = 2.0 / (CAP * owners * pair_count)

    def load(kind, c):
        cols = pl.ds(pl.multiple_of(c * width, 128), width)
        source, target = (
            (gate_hbm.at[0, cols, :], gate_buf.at[c]),
            (up_hbm.at[0, cols, :], up_buf.at[c]),
            (down_hbm.at[0, :, cols], down_buf.at[c]),
        )[kind]
        return pltpu.make_async_copy(source, target, load_sem.at[kind, c])

    for c in range(CHUNKS):
        load(0, c).start()
        load(1, c).start()
    for c in range(CHUNKS):
        load(2, c).start()

    barrier = pltpu.get_barrier_semaphore()
    for i in range(1, owners):
        pl.semaphore_signal(
            barrier, inc=1, device_id=(lax.rem(me + i, owners), place), device_id_type=MESH
        )
    for i in range(1, pair_count):
        pl.semaphore_signal(
            barrier, inc=1, device_id=(me, lax.rem(place + i, pair_count)), device_id_type=MESH
        )

    slot = lax.broadcasted_iota(jnp.int32, (tok_count, slots), 1)
    target = (slot // CAP) * per_owner
    picked = jnp.zeros((tok_count, slots), jnp.float32)
    slot_weight = jnp.zeros((tok_count, slots), jnp.float32)
    for k in range(ids_ref.shape[1]):
        hit = ids_ref[:, k : k + 1] == target
        picked = jnp.where(hit, 1.0, picked)
        slot_weight = jnp.where(hit, weight_ref[:, k : k + 1], slot_weight)
    earlier = lax.broadcasted_iota(jnp.int32, (tok_count, tok_count), 0) > lax.broadcasted_iota(
        jnp.int32, (tok_count, tok_count), 1
    )
    before = jnp.dot(
        earlier.astype(jnp.float32).astype(jnp.bfloat16),
        picked.astype(jnp.bfloat16),
        preferred_element_type=jnp.float32,
    )
    rank = (slot % CAP).astype(jnp.float32)
    marks = jnp.where(before == rank, picked, 0.0)
    slot_weight = slot_weight * marks
    weight_high = slot_weight.astype(jnp.bfloat16)
    weight_low = (slot_weight - weight_high.astype(jnp.float32)).astype(jnp.bfloat16)
    marks_by_slot = marks.T.astype(jnp.bfloat16)

    pl.semaphore_wait(barrier, owners + pair_count - 2)

    def there(c, i):
        peer = lax.rem(me + i, owners)
        return pltpu.make_async_remote_copy(
            src_ref=outgoing.at[c, pl.ds(pl.multiple_of(peer * CAP, CAP), CAP), :],
            dst_ref=arrived.at[c, pl.ds(pl.multiple_of(me * CAP, CAP), CAP), :],
            send_sem=there_send.at[c, i - 1],
            recv_sem=there_recv.at[c, i - 1],
            device_id=(peer, place),
            device_id_type=MESH,
        )

    def back(c, i):
        peer = lax.rem(me + i, owners)
        return pltpu.make_async_remote_copy(
            src_ref=results.at[c, pl.ds(pl.multiple_of(peer * CAP, CAP), CAP), :],
            dst_ref=returned.at[c, pl.ds(pl.multiple_of(me * CAP, CAP), CAP), :],
            send_sem=back_send.at[c, i - 1],
            recv_sem=back_recv.at[c, i - 1],
            device_id=(peer, place),
            device_id_type=MESH,
        )

    mine = pl.ds(pl.multiple_of(me * CAP, CAP), CAP)

    for c in range(CHUNKS):
        outgoing[c] = jnp.dot(
            marks_by_slot,
            tokens_ref[:, c * width : (c + 1) * width],
            preferred_element_type=jnp.float32,
        ).astype(jnp.bfloat16)
        for i in range(1, owners):
            there(c, i).start()
        arrived[c, mine, :] = outgoing[c, mine, :]

    gate_acc[...] = jnp.zeros_like(gate_acc)
    up_acc[...] = jnp.zeros_like(up_acc)

    def project(c, carry):
        load(0, c).wait()
        load(1, c).wait()
        for i in range(1, owners):
            there(c, i).wait_recv()
        rows = arrived[c]
        gate_acc[...] += jnp.dot(rows, gate_buf[c], preferred_element_type=jnp.float32)
        up_acc[...] += jnp.dot(rows, up_buf[c], preferred_element_type=jnp.float32)
        return carry

    lax.fori_loop(0, CHUNKS, project, 0)

    gate = gate_acc[...]
    hidden = (gate / (1.0 + jnp.exp(-gate)) * up_acc[...]).astype(jnp.bfloat16)
    block = pl.ds(pl.multiple_of(place * slots, CAP), slots)
    hidden_all[block, :] = hidden
    square = hidden.astype(jnp.float32)
    square = jnp.sum((square * square).reshape(slots // 8, 8, FF), axis=0)
    total = square[:, 0:128]
    for part in range(1, FF // 128):
        total = total + square[:, part * 128 : (part + 1) * 128]
    squares[place] = total

    def shared(kind, i):
        ref = (
            hidden_all.at[block, 0:PANEL],
            squares.at[place],
            hidden_all.at[block, PANEL:FF],
        )[kind]
        return pltpu.make_async_remote_copy(
            src_ref=ref,
            dst_ref=ref,
            send_sem=pair_send.at[kind, i - 1],
            recv_sem=pair_recv.at[kind, i - 1],
            device_id=(me, lax.rem(place + i, pair_count)),
            device_id_type=MESH,
        )

    for kind in range(3):
        for i in range(1, pair_count):
            shared(kind, i).start()

    def project_down(c, carry):
        load(2, c).wait()
        results[c] = jnp.dot(
            hidden_all[block, :], down_buf[c], preferred_element_type=jnp.float32
        ).astype(jnp.bfloat16)
        for i in range(1, owners):
            back(c, i).start()
        returned[c, mine, :] = results[c, mine, :]
        return carry

    lax.fori_loop(0, CHUNKS, project_down, 0)

    for i in range(1, pair_count):
        shared(0, i).wait_recv()
        shared(1, i).wait_recv()
    damping = jnp.sum(jnp.sum(squares[...], axis=0), axis=0, keepdims=True)
    damping = jnp.sum(damping, axis=1, keepdims=True) * (0.01 * hess_scale / FF)
    row_ids = lax.broadcasted_iota(jnp.int32, (PANEL, PANEL), 0)
    column_ids = lax.broadcasted_iota(jnp.int32, (PANEL, PANEL), 1)
    diagonal = row_ids == column_ids
    lead = hidden_all[:, 0:PANEL]
    corner = lax.dot_general(
        lead, lead, (((0,), (0,)), ((), ())), preferred_element_type=jnp.float32
    )
    elim[...] = corner * hess_scale + jnp.where(diagonal, damping, 0.0)
    row_number = lax.broadcasted_iota(jnp.int32, (PANEL, 1), 0)
    lane_number = lax.broadcasted_iota(jnp.int32, (1, PANEL), 1)

    def eliminate(j, carry):
        rest = elim[...]
        row = elim[pl.ds(j, 1), :]
        lane = lane_number == j
        pivot = jnp.sum(jnp.where(lane, row, 0.0), axis=1, keepdims=True)
        column = jnp.sum(jnp.where(lane, rest, 0.0), axis=1, keepdims=True)
        below = row_number > j
        factor = jnp.where(below, column * (1.0 / pivot), 0.0)
        elim[...] = jnp.where(lane, jnp.where(below, -factor, column), rest - factor * row)
        return carry

    lax.fori_loop(0, PANEL, eliminate, 0)
    done = elim[...]
    pivots = jnp.sum(jnp.where(diagonal, done, 0.0), axis=1, keepdims=True)
    inverse = jnp.where(row_ids > column_ids, done, jnp.where(diagonal, 1.0, 0.0))
    inverse = inverse * lax.rsqrt(pivots)

    for i in range(1, pair_count):
        shared(2, i).wait_recv()
    start, offset = window_of(place, share)
    hess_buf[...] = (
        lax.dot_general(
            hidden_all[:, pl.ds(pl.multiple_of(start, 128), window)],
            hidden_all[...],
            (((0,), (0,)), ((), ())),
            preferred_element_type=jnp.float32,
        )
        * hess_scale
    )
    my_rows = pl.ds(pl.multiple_of(offset, 8), share)
    store_hessian = pltpu.make_async_copy(
        hess_buf.at[my_rows, :], hessian_hbm.at[0], store_sem.at[CHUNKS]
    )
    store_hessian.start()
    own_ids = place * share + lax.broadcasted_iota(jnp.int32, (share, PANEL), 0)
    own_columns = lax.broadcasted_iota(jnp.int32, (share, PANEL), 1)
    leading = hess_buf[my_rows, 0:PANEL] + jnp.where(own_ids == own_columns, damping, 0.0)
    panel_buf[...] = lax.dot_general(
        leading,
        inverse,
        (((1,), (1,)), ((), ())),
        precision=HIGHEST,
        preferred_element_type=jnp.float32,
    )
    store_panel = pltpu.make_async_copy(panel_buf, panel_hbm.at[0], store_sem.at[CHUNKS + 1])
    store_panel.start()

    def store(c):
        cols = pl.ds(pl.multiple_of(c * width, 128), width)
        return pltpu.make_async_copy(mixed.at[c], combined_hbm.at[:, cols], store_sem.at[c])

    for c in range(CHUNKS):
        for i in range(1, owners):
            back(c, i).wait_recv()
        rows = returned[c]
        mixed[c] = (
            jnp.dot(weight_high, rows, preferred_element_type=jnp.float32)
            + jnp.dot(weight_low, rows, preferred_element_type=jnp.float32)
        ).astype(jnp.bfloat16)
        store(c).start()

    for c in range(CHUNKS):
        for i in range(1, owners):
            there(c, i).wait_send()
            back(c, i).wait_send()
    for i in range(1, pair_count):
        for kind in range(3):
            shared(kind, i).wait_send()
    store_hessian.wait()
    store_panel.wait()
    for c in range(CHUNKS):
        store(c).wait()


def per_device(
    owners, pair_count, tokens, expert_ids, route_weight, gate_weight, up_weight, down_weight
):
    tok_count, model_width = tokens.shape
    width = model_width // CHUNKS
    slots = owners * CAP
    share = FF // pair_count
    reach = max(window_of(p, share)[1] for p in range(pair_count)) + share
    window = -(-reach // 128) * 128
    vmem = pl.BlockSpec(memory_space=pltpu.VMEM)
    hbm = pl.BlockSpec(memory_space=pl.ANY)
    bf16, f32 = jnp.bfloat16, jnp.float32
    dma = pltpu.SemaphoreType.DMA
    return pl.pallas_call(
        functools.partial(kernel, owners, pair_count, window),
        out_shape=(
            jax.ShapeDtypeStruct((tok_count, model_width), bf16),
            jax.ShapeDtypeStruct((1, share, FF), f32),
            jax.ShapeDtypeStruct((1, share, PANEL), f32),
        ),
        in_specs=[vmem, vmem, vmem, hbm, hbm, hbm],
        out_specs=(hbm, hbm, hbm),
        scratch_shapes=[
            pltpu.VMEM((CHUNKS, width, FF), bf16),
            pltpu.VMEM((CHUNKS, width, FF), bf16),
            pltpu.VMEM((CHUNKS, FF, width), bf16),
            pltpu.VMEM((CHUNKS, slots, width), bf16),
            pltpu.VMEM((CHUNKS, slots, width), bf16),
            pltpu.VMEM((CHUNKS, slots, width), bf16),
            pltpu.VMEM((CHUNKS, slots, width), bf16),
            pltpu.VMEM((CHUNKS, tok_count, width), bf16),
            pltpu.VMEM((slots, FF), f32),
            pltpu.VMEM((slots, FF), f32),
            pltpu.VMEM((pair_count * slots, FF), bf16),
            pltpu.VMEM((pair_count, 8, 128), f32),
            pltpu.VMEM((PANEL, PANEL), f32),
            pltpu.VMEM((window, FF), f32),
            pltpu.VMEM((share, PANEL), f32),
            dma((3, CHUNKS)),
            dma((CHUNKS, owners - 1)),
            dma((CHUNKS, owners - 1)),
            dma((CHUNKS, owners - 1)),
            dma((CHUNKS, owners - 1)),
            dma((3, pair_count - 1)),
            dma((3, pair_count - 1)),
            dma((CHUNKS + 2,)),
        ],
        compiler_params=pltpu.CompilerParams(
            collective_id=0, has_side_effects=True, vmem_limit_bytes=56 * 1024 * 1024
        ),
        cost_estimate=pl.CostEstimate(
            flops=2 * slots * model_width * FF * 3,
            bytes_accessed=3 * 2 * model_width * FF,
            transcendentals=slots * FF,
        ),
        name="experts",
    )(tokens, expert_ids, route_weight, gate_weight, up_weight, down_weight)


def solution(mesh):
    in_specs = (
        P(("expert", "pair"), None),
        P(("expert", "pair"), None),
        P(("expert", "pair"), None),
        P("expert", None, None),
        P("expert", None, None),
        P("expert", None, None),
    )
    out_specs = (P(("expert", "pair"), None), P("expert", "pair", None), P("expert", "pair", None))
    return jax.shard_map(
        functools.partial(per_device, mesh.shape["expert"], mesh.shape["pair"]),
        mesh=mesh,
        in_specs=in_specs,
        out_specs=out_specs,
        check_vma=False,
    )
```

time: 178 us -> 60.2 us (0.34)
  waiting for transfers between devices: 78.8 us -> 0 us
  Pallas kernels: 0 us -> 50.6 us
  other arithmetic: 36.4 us -> 0 us
  matrix products: 14.9 us -> 0 us
  between operations: 15 us -> 0.64 us
  local copies, waits for them, and re-layouts: 22.7 us -> 8.57 us
  starting transfers between devices: 9.08 us -> 0 us
    pallas_call x0 -> x1, Pallas kernels: none -> 50.6 us  [per_device(): pl.pallas_call(functools.partial(kernel, owners, pair_count, window), out...]
    psum x1 -> x0, waiting for transfers between devices: 49 us -> none  [per_device(): whole_sum = lax.psum(local_sum, 'pair')]
    all_to_all x2 -> x0, waiting for transfers between devices: 29.8 us -> none  [the longest x1 15.1 us: per_device(): lax.all_to_all(results, 'expert', split_axis=0, concat_axis=0, tiled=True)]
    another operation x6 -> x0, other arithmetic: 23 us -> none  [the longest x3 12.4 us: per_device(): jnp.linalg.cholesky(corner + damping * jnp.eye(PANEL, dtype=jnp.float32))]
    gather x9 -> x0, local copies, waits for them, and re-layouts: 18.8 us -> none  [the longest x8 16.6 us: per_device(): fetched = jnp.take(returned_flat, slot_index[:, column_index], axis=0)]
    dot_general x4 -> x0, matrix products: 13.1 us -> none  [the longest x1 4.75 us: swiglu_rows(): jnp.dot(hidden, down_matrix, preferred_element_type=jnp.float32)]
    all_to_all x2 -> x0, starting transfers between devices: 9.04 us -> none  [the longest x1 5.17 us: per_device(): lax.all_to_all(outgoing, 'expert', split_axis=0, concat_axis=0, tiled=True)]
    unnamed x9 -> x5, local copies, waits for them, and re-layouts: 0.93 us -> 8.57 us
  transfers between devices with their start and end apart: 3 -> 0, of which waited for: 3 -> 0; matrix products, arithmetic and copies ran while one was open for 16% -> 0% of each run, Pallas kernels for 0% -> 0%
where the time goes in v1:
time: 60.2 us; the launch traced here: 59.9 us
  Pallas kernels  50.6 us (84%)
  local copies, waits for them, and re-layouts  8.57 us (14%)
  between operations  0.64 us (1%)
    pallas_call x1, Pallas kernels, per_device(): pl.pallas_call(functools.partial(kernel, owners, pair_count, window), out...  50.6 us
    unnamed x5, local copies, waits for them, and re-layouts  8.57 us

profile of v1, /device:TPU:0, one launch (start us, length us, event | category | flops | bytes accessed | tf_op | source)
XLA Modules:
  0.0 59.9 jit_solution(3824718664395945628)
XLA Ops:
  0.6 1.4 %copy.9.ids_ref = s32[128,8]{1,0:T(8,128)} copy(s32[128,8]{0,1:T(8,128)} %param.7) | data formatting | bytes 8192 | tf_op args[1]
  2.0 1.4 %copy.10.weight_ref = f32[128,8]{1,0:T(8,128)} copy(f32[128,8]{0,1:T(8,128)} %param.8) | data formatting | bytes 8192 | tf_op args[2]
  3.5 50.6 %experts.1 = (bf16[128,4096]{1,0:T(8,128)(2,1)}, f32[1,192,768]{2,1,0:T(8,128)}, f32[1,192,128]{2,1,0:T(8,128)}) custom-call(bf16[128,4096]{1,0:T(8,128)(2,1)} %tokens_ref.1, s32[128,8]{1,0:T(8,128)} %copy.9.ids_ref, f32[128,8]{1,0:T(8,128)} %copy.10.weight_ref, bf16[1,4096,768]{2,1,0:T(8,128)(2,1)} %gate_hbm.1, bf16[1,4096,768]{2,1,0:T(8,128)(2,1)} %up_hbm.1, ...), custom_call_target="tpu_custom_call" | custom-call | flops 2415919104 | bytes 18874368 | tf_op jit(solution)/shard_map/experts/pallas_call | solution.py:314
  54.1 2.3 %copy.14 = bf16[128,4096]{1,0:T(8,128)(2,1)} copy(bf16[128,4096]{1,0:T(8,128)(2,1)} %get-tuple-element.6) | data formatting | bytes 2097152
  56.4 1.9 %copy.15 = f32[1,192,768]{2,1,0:T(8,128)} copy(f32[1,192,768]{2,1,0:T(8,128)} %get-tuple-element.7) | data formatting | bytes 1179648
  58.3 1.5 %copy.16 = f32[1,192,128]{2,1,0:T(8,128)} copy(f32[1,192,128]{2,1,0:T(8,128)} %get-tuple-element.8) | data formatting | bytes 196608

commit v2 on v1

--- a/solution.py
+++ b/solution.py
@@ -31,7 +31,8 @@
     gate_hbm,
     up_hbm,
     down_hbm,
-    combined_hbm,
+    returned,
+    mix_hbm,
     hessian_hbm,
     panel_hbm,
     gate_buf,
@@ -40,8 +41,7 @@
     outgoing,
     arrived,
     results,
-    returned,
-    mixed,
+    mix_buf,
     gate_acc,
     up_acc,
     hidden_all,
@@ -56,6 +56,8 @@
     back_recv,
     pair_send,
     pair_recv,
+    pass_send,
+    pass_recv,
     store_sem,
 ):
     me = lax.axis_index("expert")
@@ -92,28 +94,25 @@
             barrier, inc=1, device_id=(me, lax.rem(place + i, pair_count)), device_id_type=MESH
         )
 
-    slot = lax.broadcasted_iota(jnp.int32, (tok_count, slots), 1)
+    slot = lax.broadcasted_iota(jnp.int32, (slots, tok_count), 0)
     target = (slot // CAP) * per_owner
-    picked = jnp.zeros((tok_count, slots), jnp.float32)
-    slot_weight = jnp.zeros((tok_count, slots), jnp.float32)
-    for k in range(ids_ref.shape[1]):
-        hit = ids_ref[:, k : k + 1] == target
+    picked = jnp.zeros((slots, tok_count), jnp.float32)
+    slot_weight = jnp.zeros((slots, tok_count), jnp.float32)
+    for k in range(ids_ref.shape[0]):
+        hit = ids_ref[k : k + 1, :] == target
         picked = jnp.where(hit, 1.0, picked)
-        slot_weight = jnp.where(hit, weight_ref[:, k : k + 1], slot_weight)
-    earlier = lax.broadcasted_iota(jnp.int32, (tok_count, tok_count), 0) > lax.broadcasted_iota(
+        slot_weight = jnp.where(hit, weight_ref[k : k + 1, :], slot_weight)
+    earlier = lax.broadcasted_iota(jnp.int32, (tok_count, tok_count), 0) < lax.broadcasted_iota(
         jnp.int32, (tok_count, tok_count), 1
     )
     before = jnp.dot(
+        picked.astype(jnp.bfloat16),
         earlier.astype(jnp.float32).astype(jnp.bfloat16),
-        picked.astype(jnp.bfloat16),
         preferred_element_type=jnp.float32,
     )
     rank = (slot % CAP).astype(jnp.float32)
     marks = jnp.where(before == rank, picked, 0.0)
-    slot_weight = slot_weight * marks
-    weight_high = slot_weight.astype(jnp.bfloat16)
-    weight_low = (slot_weight - weight_high.astype(jnp.float32)).astype(jnp.bfloat16)
-    marks_by_slot = marks.T.astype(jnp.bfloat16)
+    marks_by_slot = marks.astype(jnp.bfloat16)
 
     pl.semaphore_wait(barrier, owners + pair_count - 2)
 
@@ -139,6 +138,11 @@
             device_id_type=MESH,
         )
 
+    def keep(c):
+        return pltpu.make_async_copy(
+            results.at[c, mine, :], returned.at[c, mine, :], store_sem.at[c]
+        )
+
     mine = pl.ds(pl.multiple_of(me * CAP, CAP), CAP)
 
     for c in range(CHUNKS):
@@ -150,6 +154,13 @@
         for i in range(1, owners):
             there(c, i).start()
         arrived[c, mine, :] = outgoing[c, mine, :]
+
+    weights = (slot_weight * marks).T
+    weight_high = weights.astype(jnp.bfloat16)
+    mix_buf[0] = weight_high
+    mix_buf[1] = (weights - weight_high.astype(jnp.float32)).astype(jnp.bfloat16)
+    store_mix = pltpu.make_async_copy(mix_buf, mix_hbm, store_sem.at[CHUNKS + 2])
+    store_mix.start()
 
     gate_acc[...] = jnp.zeros_like(gate_acc)
     up_acc[...] = jnp.zeros_like(up_acc)
@@ -181,7 +192,6 @@
         ref = (
             hidden_all.at[block, 0:PANEL],
             squares.at[place],
-            hidden_all.at[block, PANEL:FF],
         )[kind]
         return pltpu.make_async_remote_copy(
             src_ref=ref,
@@ -192,9 +202,40 @@
             device_id_type=MESH,
         )
 
-    for kind in range(3):
+    def passing(step, side, number):
+        toward = (1, -1)[side]
+        ref = hidden_all.at[pl.ds(pl.multiple_of(number * slots, CAP), slots), PANEL:FF]
+        return pltpu.make_async_remote_copy(
+            src_ref=ref,
+            dst_ref=ref,
+            send_sem=pass_send.at[side, step - 1],
+            recv_sem=pass_recv.at[side, step - 1],
+            device_id=(me, lax.rem(place + toward + pair_count, pair_count)),
+            device_id_type=MESH,
+        )
+
+    def each_send(step, action):
+        @pl.when(jnp.logical_and(place >= step - 1, place < pair_count - 1))
+        def _():
+            action(passing(step, 0, place - step + 1))
+
+        @pl.when(jnp.logical_and(place <= pair_count - step, place > 0))
+        def _():
+            action(passing(step, 1, place + step - 1))
+
+    def receive(step):
+        @pl.when(place >= step)
+        def _():
+            passing(step, 0, place - step).wait_recv()
+
+        @pl.when(place < pair_count - step)
+        def _():
+            passing(step, 1, place + step).wait_recv()
+
+    for kind in range(2):
         for i in range(1, pair_count):
             shared(kind, i).start()
+    each_send(1, lambda copy: copy.start())
 
     def project_down(c, carry):
         load(2, c).wait()
@@ -203,7 +244,7 @@
         ).astype(jnp.bfloat16)
         for i in range(1, owners):
             back(c, i).start()
-        returned[c, mine, :] = results[c, mine, :]
+        keep(c).start()
         return carry
 
     lax.fori_loop(0, CHUNKS, project_down, 0)
@@ -224,25 +265,47 @@
     row_number = lax.broadcasted_iota(jnp.int32, (PANEL, 1), 0)
     lane_number = lax.broadcasted_iota(jnp.int32, (1, PANEL), 1)
 
-    def eliminate(j, carry):
+    def eliminate(pair, carry):
+        j = 2 * pair
         rest = elim[...]
-        row = elim[pl.ds(j, 1), :]
-        lane = lane_number == j
-        pivot = jnp.sum(jnp.where(lane, row, 0.0), axis=1, keepdims=True)
-        column = jnp.sum(jnp.where(lane, rest, 0.0), axis=1, keepdims=True)
-        below = row_number > j
-        factor = jnp.where(below, column * (1.0 / pivot), 0.0)
-        elim[...] = jnp.where(lane, jnp.where(below, -factor, column), rest - factor * row)
+        row0 = elim[pl.ds(j, 1), :]
+        row1 = elim[pl.ds(j + 1, 1), :]
+        lane0 = lane_number == j
+        lane1 = lane_number == j + 1
+        pivot0 = jnp.sum(jnp.where(lane0, row0, 0.0), axis=1, keepdims=True)
+        cross = jnp.sum(jnp.where(lane1, row0, 0.0), axis=1, keepdims=True)
+        pivot1 = jnp.sum(jnp.where(lane1, row1, 0.0), axis=1, keepdims=True)
+        column0 = jnp.sum(jnp.where(lane0, rest, 0.0), axis=1, keepdims=True)
+        column1 = jnp.sum(jnp.where(lane1, rest, 0.0), axis=1, keepdims=True)
+        below = row_number > j + 1
+        scale0 = 1.0 / pivot0
+        ratio = cross * scale0
+        pivot1 = pivot1 - ratio * cross
+        scale1 = 1.0 / pivot1
+        factor0 = jnp.where(below, column0 * scale0, 0.0)
+        factor1 = jnp.where(below, (column1 - factor0 * cross) * scale1, 0.0)
+        next1 = jnp.where(lane0, -ratio, row1 - ratio * row0)
+        take0 = jnp.where(lane0, 1.0, jnp.where(lane1, 0.0, row0))
+        take1 = jnp.where(lane1, 1.0, next1)
+        cleared = jnp.logical_and(jnp.logical_or(lane0, lane1), below)
+        elim[...] = jnp.where(cleared, 0.0, rest) - factor0 * take0 - factor1 * take1
+        elim[pl.ds(j + 1, 1), :] = jnp.where(lane1, pivot1, next1)
         return carry
 
-    lax.fori_loop(0, PANEL, eliminate, 0)
+    first = 0
+    for step in range(1, pair_count):
+        last = PANEL // 2 if step == pair_count - 1 else min(PANEL // 2, 28 * step - 12)
+        lax.fori_loop(first, last, eliminate, 0)
+        first = last
+        if step < pair_count - 1:
+            receive(step)
+            each_send(step + 1, lambda copy: copy.start())
     done = elim[...]
     pivots = jnp.sum(jnp.where(diagonal, done, 0.0), axis=1, keepdims=True)
     inverse = jnp.where(row_ids > column_ids, done, jnp.where(diagonal, 1.0, 0.0))
     inverse = inverse * lax.rsqrt(pivots)
 
-    for i in range(1, pair_count):
-        shared(2, i).wait_recv()
+    receive(pair_count - 1)
     start, offset = window_of(place, share)
     hess_buf[...] = (
         lax.dot_general(
@@ -271,31 +334,32 @@
     store_panel = pltpu.make_async_copy(panel_buf, panel_hbm.at[0], store_sem.at[CHUNKS + 1])
     store_panel.start()
 
-    def store(c):
-        cols = pl.ds(pl.multiple_of(c * width, 128), width)
-        return pltpu.make_async_copy(mixed.at[c], combined_hbm.at[:, cols], store_sem.at[c])
-
     for c in range(CHUNKS):
         for i in range(1, owners):
             back(c, i).wait_recv()
-        rows = returned[c]
-        mixed[c] = (
-            jnp.dot(weight_high, rows, preferred_element_type=jnp.float32)
-            + jnp.dot(weight_low, rows, preferred_element_type=jnp.float32)
-        ).astype(jnp.bfloat16)
-        store(c).start()
-
+        keep(c).wait()
     for c in range(CHUNKS):
         for i in range(1, owners):
             there(c, i).wait_send()
             back(c, i).wait_send()
     for i in range(1, pair_count):
-        for kind in range(3):
+        for kind in range(2):
             shared(kind, i).wait_send()
     store_hessian.wait()
+    for step in range(1, pair_count):
+        each_send(step, lambda copy: copy.wait_send())
     store_panel.wait()
-    for c in range(CHUNKS):
-        store(c).wait()
+    store_mix.wait()
+
+
+def combine(returned_ref, mix_ref, hessian_ref, panel_ref, combined_ref, hessian_out, panel_out):
+    rows = returned_ref[0]
+    combined_ref[...] = (
+        jnp.dot(mix_ref[0], rows, preferred_element_type=jnp.float32)
+        + jnp.dot(mix_ref[1], rows, preferred_element_type=jnp.float32)
+    ).astype(jnp.bfloat16)
+    hessian_out[...] = hessian_ref[...]
+    panel_out[...] = panel_ref[...]
 
 
 def per_device(
@@ -311,15 +375,16 @@
     hbm = pl.BlockSpec(memory_space=pl.ANY)
     bf16, f32 = jnp.bfloat16, jnp.float32
     dma = pltpu.SemaphoreType.DMA
-    return pl.pallas_call(
+    returned, mix, hessian, panel = pl.pallas_call(
         functools.partial(kernel, owners, pair_count, window),
         out_shape=(
-            jax.ShapeDtypeStruct((tok_count, model_width), bf16),
+            jax.ShapeDtypeStruct((CHUNKS, slots, width), bf16),
+            jax.ShapeDtypeStruct((2, tok_count, slots), bf16),
             jax.ShapeDtypeStruct((1, share, FF), f32),
             jax.ShapeDtypeStruct((1, share, PANEL), f32),
         ),
         in_specs=[vmem, vmem, vmem, hbm, hbm, hbm],
-        out_specs=(hbm, hbm, hbm),
+        out_specs=(hbm, hbm, hbm, hbm),
         scratch_shapes=[
             pltpu.VMEM((CHUNKS, width, FF), bf16),
             pltpu.VMEM((CHUNKS, width, FF), bf16),
@@ -327,8 +392,7 @@
             pltpu.VMEM((CHUNKS, slots, width), bf16),
             pltpu.VMEM((CHUNKS, slots, width), bf16),
             pltpu.VMEM((CHUNKS, slots, width), bf16),
-            pltpu.VMEM((CHUNKS, slots, width), bf16),
-            pltpu.VMEM((CHUNKS, tok_count, width), bf16),
+            pltpu.VMEM((2, tok_count, slots), bf16),
             pltpu.VMEM((slots, FF), f32),
             pltpu.VMEM((slots, FF), f32),
             pltpu.VMEM((pair_count * slots, FF), bf16),
@@ -341,9 +405,11 @@
             dma((CHUNKS, owners - 1)),
             dma((CHUNKS, owners - 1)),
             dma((CHUNKS, owners - 1)),
-            dma((3, pair_count - 1)),
-            dma((3, pair_count - 1)),
-            dma((CHUNKS + 2,)),
+            dma((2, pair_count - 1)),
+            dma((2, pair_count - 1)),
+            dma((2, pair_count - 1)),
+            dma((2, pair_count - 1)),
+            dma((CHUNKS + 3,)),
         ],
         compiler_params=pltpu.CompilerParams(
             collective_id=0, has_side_effects=True, vmem_limit_bytes=56 * 1024 * 1024
@@ -354,7 +420,36 @@
             transcendentals=slots * FF,
         ),
         name="experts",
-    )(tokens, expert_ids, route_weight, gate_weight, up_weight, down_weight)
+    )(tokens, expert_ids.T, route_weight.T, gate_weight, up_weight, down_weight)
+    strip = share // CHUNKS
+    hessian_spec = pl.BlockSpec((1, strip, FF), lambda c: (0, c, 0))
+    panel_spec = pl.BlockSpec((1, strip, PANEL), lambda c: (0, c, 0))
+    return pl.pallas_call(
+        combine,
+        grid=(CHUNKS,),
+        out_shape=(
+            jax.ShapeDtypeStruct((tok_count, model_width), bf16),
+            jax.ShapeDtypeStruct((1, share, FF), f32),
+            jax.ShapeDtypeStruct((1, share, PANEL), f32),
+        ),
+        in_specs=[
+            pl.BlockSpec((1, slots, width), lambda c: (c, 0, 0)),
+            pl.BlockSpec((2, tok_count, slots), lambda c: (0, 0, 0)),
+            hessian_spec,
+            panel_spec,
+        ],
+        out_specs=(
+            pl.BlockSpec((tok_count, width), lambda c: (0, c)),
+            hessian_spec,
+            panel_spec,
+        ),
+        cost_estimate=pl.CostEstimate(
+            flops=4 * tok_count * slots * model_width,
+            bytes_accessed=4 * slots * model_width + 8 * share * (FF + PANEL),
+            transcendentals=0,
+        ),
+        name="combine",
+    )(returned, mix, hessian, panel)
 
 
 def solution(mesh):

time: 60.2 us -> 46.2 us (0.77)
  local copies, waits for them, and re-layouts: 8.57 us -> 0 us
  Pallas kernels: 50.6 us -> 45.4 us
    pallas_call x1, Pallas kernels: 50.6 us -> 41.2 us  [per_device(): pl.pallas_call(functools.partial(kernel, owners, pair_count, window), out...]
    unnamed x5 -> x0, local copies, waits for them, and re-layouts: 8.57 us -> none
    pallas_call x0 -> x1, Pallas kernels: none -> 4.14 us  [per_device(): pl.pallas_call(combine, grid=(CHUNKS,), out_shape=(jax.ShapeDtypeStruct((...]
where the time goes in v2:
time: 46.2 us; the launch traced here: 46 us
  Pallas kernels  45.4 us (98%)
  between operations  0.64 us (1%)
    pallas_call x1, Pallas kernels, per_device(): pl.pallas_call(functools.partial(kernel, owners, pair_count, window), out...  41.2 us
    pallas_call x1, Pallas kernels, per_device(): pl.pallas_call(combine, grid=(CHUNKS,), out_shape=(jax.ShapeDtypeStruct((...  4.14 us

profile of v2, /device:TPU:0, one launch (start us, length us, event | category | flops | bytes accessed | tf_op | source)
XLA Modules:
  0.0 46.0 jit_solution(89306731670971777)
XLA Ops:
  0.6 41.2 %experts.1 = (bf16[4,128,1024]{2,1,0:T(8,128)(2,1)}, bf16[2,128,128]{2,1,0:T(8,128)(2,1)}, f32[1,192,768]{2,1,0:T(8,128)}, f32[1,192,128]{2,1,0:T(8,128)}) custom-call(bf16[128,4096]{1,0:T(8,128)(2,1)} %tokens_ref.1, s32[8,128]{1,0:T(8,128)} %bitcast.2, f32[8,128]{1,0:T(8,128)} %bitcast.3, bf16[1,4096,768]{2,1,0:T(8,128)(2,1)} %gate_hbm.1, ...), custom_call_target="tpu_custom_call" | custom-call | flops 2415919104 | bytes 18874368 | tf_op jit(solution)/shard_map/experts/pallas_call | solution.py:378
  41.9 4.1 %combine.1 = (bf16[128,4096]{1,0:T(8,128)(2,1)}, f32[1,192,768]{2,1,0:T(8,128)}, f32[1,192,128]{2,1,0:T(8,128)}) custom-call(bf16[4,128,1024]{2,1,0:T(8,128)(2,1)} %get-tuple-element.7.returned_ref, bf16[2,128,128]{2,1,0:T(8,128)(2,1)} %get-tuple-element.8.mix_ref, f32[1,192,768]{2,1,0:T(8,128)} %get-tuple-element.9.hessian_ref, ...), custom_call_target="tpu_custom_call" | custom-call | flops 268435456 | bytes 3473408 | tf_op jit(solution)/shard_map/combine/pallas_call | solution.py:427

commit v3 on v2

--- a/solution.py
+++ b/solution.py
@@ -12,6 +12,7 @@
 PANEL = 128
 CAP = 16
 CHUNKS = 4
+GROUP = 4
 MESH = pl.DeviceIdType.MESH
 HIGHEST = lax.Precision.HIGHEST
 
@@ -265,36 +266,44 @@
     row_number = lax.broadcasted_iota(jnp.int32, (PANEL, 1), 0)
     lane_number = lax.broadcasted_iota(jnp.int32, (1, PANEL), 1)
 
-    def eliminate(pair, carry):
-        j = 2 * pair
+    def eliminate(number, carry):
+        j = GROUP * number
+        group = range(GROUP)
         rest = elim[...]
-        row0 = elim[pl.ds(j, 1), :]
-        row1 = elim[pl.ds(j + 1, 1), :]
-        lane0 = lane_number == j
-        lane1 = lane_number == j + 1
-        pivot0 = jnp.sum(jnp.where(lane0, row0, 0.0), axis=1, keepdims=True)
-        cross = jnp.sum(jnp.where(lane1, row0, 0.0), axis=1, keepdims=True)
-        pivot1 = jnp.sum(jnp.where(lane1, row1, 0.0), axis=1, keepdims=True)
-        column0 = jnp.sum(jnp.where(lane0, rest, 0.0), axis=1, keepdims=True)
-        column1 = jnp.sum(jnp.where(lane1, rest, 0.0), axis=1, keepdims=True)
-        below = row_number > j + 1
-        scale0 = 1.0 / pivot0
-        ratio = cross * scale0
-        pivot1 = pivot1 - ratio * cross
-        scale1 = 1.0 / pivot1
-        factor0 = jnp.where(below, column0 * scale0, 0.0)
-        factor1 = jnp.where(below, (column1 - factor0 * cross) * scale1, 0.0)
-        next1 = jnp.where(lane0, -ratio, row1 - ratio * row0)
-        take0 = jnp.where(lane0, 1.0, jnp.where(lane1, 0.0, row0))
-        take1 = jnp.where(lane1, 1.0, next1)
-        cleared = jnp.logical_and(jnp.logical_or(lane0, lane1), below)
-        elim[...] = jnp.where(cleared, 0.0, rest) - factor0 * take0 - factor1 * take1
-        elim[pl.ds(j + 1, 1), :] = jnp.where(lane1, pivot1, next1)
+        rows = [elim[pl.ds(j + m, 1), :] for m in group]
+        lanes = [lane_number == j + m for m in group]
+        below = row_number > j + GROUP - 1
+
+        def pick(values, m):
+            return jnp.sum(jnp.where(lanes[m], values, 0.0), axis=1, keepdims=True)
+
+        cross = {(m, k): pick(rows[m], k) for m in group for k in range(m, GROUP)}
+        columns = [jnp.where(below, pick(rest, m), 0.0) for m in group]
+        factors = []
+        for m in group:
+            scale = 1.0 / cross[m, m]
+            factors.append(columns[m] * scale)
+            for k in range(m + 1, GROUP):
+                ratio = cross[m, k] * scale
+                columns[k] = columns[k] - factors[m] * cross[m, k]
+                rows[k] = jnp.where(lanes[m], -ratio, rows[k] - ratio * rows[m])
+                for q in range(k, GROUP):
+                    cross[k, q] = cross[k, q] - ratio * cross[m, q]
+        inside = jnp.logical_and(lane_number >= j, lane_number < j + GROUP)
+        updated = jnp.where(jnp.logical_and(inside, below), 0.0, rest)
+        for m in group:
+            later = jnp.logical_and(inside, lane_number > j + m)
+            taken = jnp.where(lanes[m], 1.0, jnp.where(later, 0.0, rows[m]))
+            updated = updated - factors[m] * taken
+        elim[...] = updated
+        for m in range(1, GROUP):
+            elim[pl.ds(j + m, 1), :] = rows[m]
         return carry
 
+    groups = PANEL // GROUP
     first = 0
     for step in range(1, pair_count):
-        last = PANEL // 2 if step == pair_count - 1 else min(PANEL // 2, 28 * step - 12)
+        last = groups if step == pair_count - 1 else min(groups, 14 * step - 8)
         lax.fori_loop(first, last, eliminate, 0)
         first = last
         if step < pair_count - 1:
@@ -352,14 +361,49 @@
     store_mix.wait()
 
 
-def combine(returned_ref, mix_ref, hessian_ref, panel_ref, combined_ref, hessian_out, panel_out):
-    rows = returned_ref[0]
-    combined_ref[...] = (
-        jnp.dot(mix_ref[0], rows, preferred_element_type=jnp.float32)
-        + jnp.dot(mix_ref[1], rows, preferred_element_type=jnp.float32)
-    ).astype(jnp.bfloat16)
-    hessian_out[...] = hessian_ref[...]
-    panel_out[...] = panel_ref[...]
+def combine(
+    returned,
+    mix_ref,
+    hessian_hbm,
+    panel_hbm,
+    combined_hbm,
+    hessian_out,
+    panel_out,
+    rows_buf,
+    mixed,
+    load_sem,
+    store_sem,
+    pass_sem,
+):
+    width = returned.shape[2]
+
+    def load(c):
+        return pltpu.make_async_copy(returned.at[c], rows_buf.at[c], load_sem.at[c])
+
+    def store(c):
+        cols = pl.ds(c * width, width)
+        return pltpu.make_async_copy(mixed.at[c], combined_hbm.at[:, cols], store_sem.at[c])
+
+    passes = (
+        pltpu.make_async_copy(hessian_hbm, hessian_out, pass_sem.at[0]),
+        pltpu.make_async_copy(panel_hbm, panel_out, pass_sem.at[1]),
+    )
+    for c in range(CHUNKS):
+        load(c).start()
+    for copy in passes:
+        copy.start()
+    for c in range(CHUNKS):
+        load(c).wait()
+        rows = rows_buf[c]
+        mixed[c] = (
+            jnp.dot(mix_ref[0], rows, preferred_element_type=jnp.float32)
+            + jnp.dot(mix_ref[1], rows, preferred_element_type=jnp.float32)
+        ).astype(jnp.bfloat16)
+        store(c).start()
+    for c in range(CHUNKS):
+        store(c).wait()
+    for copy in passes:
+        copy.wait()
 
 
 def per_device(
@@ -421,28 +465,23 @@
         ),
         name="experts",
     )(tokens, expert_ids.T, route_weight.T, gate_weight, up_weight, down_weight)
-    strip = share // CHUNKS
-    hessian_spec = pl.BlockSpec((1, strip, FF), lambda c: (0, c, 0))
-    panel_spec = pl.BlockSpec((1, strip, PANEL), lambda c: (0, c, 0))
     return pl.pallas_call(
         combine,
-        grid=(CHUNKS,),
         out_shape=(
             jax.ShapeDtypeStruct((tok_count, model_width), bf16),
             jax.ShapeDtypeStruct((1, share, FF), f32),
             jax.ShapeDtypeStruct((1, share, PANEL), f32),
         ),
-        in_specs=[
-            pl.BlockSpec((1, slots, width), lambda c: (c, 0, 0)),
-            pl.BlockSpec((2, tok_count, slots), lambda c: (0, 0, 0)),
-            hessian_spec,
-            panel_spec,
+        in_specs=[hbm, vmem, hbm, hbm],
+        out_specs=(hbm, hbm, hbm),
+        scratch_shapes=[
+            pltpu.VMEM((CHUNKS, slots, width), bf16),
+            pltpu.VMEM((CHUNKS, tok_count, width), bf16),
+            dma((CHUNKS,)),
+            dma((CHUNKS,)),
+            dma((2,)),
         ],
-        out_specs=(
-            pl.BlockSpec((tok_count, width), lambda c: (0, c)),
-            hessian_spec,
-            panel_spec,
-        ),
+        compiler_params=pltpu.CompilerParams(vmem_limit_bytes=48 * 1024 * 1024),
         cost_estimate=pl.CostEstimate(
             flops=4 * tok_count * slots * model_width,
             bytes_accessed=4 * slots * model_width + 8 * share * (FF + PANEL),

time: 46.2 us -> 48.2 us (1.043)
  local copies, waits for them, and re-layouts: 0 us -> 4.01 us
  Pallas kernels: 45.4 us -> 43.2 us
    unnamed x0 -> x8, local copies, waits for them, and re-layouts: none -> 4.01 us
    pallas_call x1, Pallas kernels: 4.14 us -> 2.02 us  [per_device(): pl.pallas_call(combine, out_shape=(jax.ShapeDtypeStruct((tok_count, model...]
where the time goes in v3:
time: 48.2 us; the launch traced here: 47.9 us
  Pallas kernels  43.2 us (90%)
  local copies, waits for them, and re-layouts  4.01 us (8%)
  between operations  0.65 us (1%)
    pallas_call x1, Pallas kernels, per_device(): pl.pallas_call(functools.partial(kernel, owners, pair_count, window), out...  41.2 us
    unnamed x8, local copies, waits for them, and re-layouts  4.01 us
    pallas_call x1, Pallas kernels, per_device(): pl.pallas_call(combine, out_shape=(jax.ShapeDtypeStruct((tok_count, model...  2.02 us

profile of v3, /device:TPU:0, one launch (start us, length us, event | category | flops | bytes accessed | tf_op | source)
XLA Modules:
  0.0 47.9 jit_solution(2999437975192458861)
XLA Ops:
  0.6 41.2 %experts.1 = (bf16[4,128,1024]{2,1,0:T(8,128)(2,1)}, bf16[2,128,128]{2,1,0:T(8,128)(2,1)}, f32[1,192,768]{2,1,0:T(8,128)}, f32[1,192,128]{2,1,0:T(8,128)}) custom-call(bf16[128,4096]{1,0:T(8,128)(2,1)} %tokens_ref.1, s32[8,128]{1,0:T(8,128)} %bitcast.2, f32[8,128]{1,0:T(8,128)} %bitcast.3, bf16[1,4096,768]{2,1,0:T(8,128)(2,1)} %gate_hbm.1, ...), custom_call_target="tpu_custom_call" | custom-call | flops 2415919104 | bytes 18874368 | tf_op jit(solution)/shard_map/experts/pallas_call | solution.py:422
  41.9 0.0 copy-start
  41.9 1.2 %copy-done = bf16[4,128,1024]{2,1,0:T(8,128)(2,1)S(1)} copy-done((bf16[4,128,1024]{2,1,0:T(8,128)(2,1)S(1)}, bf16[4,128,1024]{2,1,0:T(8,128)(2,1)}, u32[]{:S(2)}) %copy-start) | copy-done | bytes 1048600
  43.1 0.0 copy-start.1
  43.1 1.1 %copy-done.1 = f32[1,192,768]{2,1,0:T(8,128)S(1)} copy-done((f32[1,192,768]{2,1,0:T(8,128)S(1)}, f32[1,192,768]{2,1,0:T(8,128)}, u32[]{:S(2)}) %copy-start.1) | copy-done | bytes 589848
  44.2 0.0 copy-start.2
  44.2 0.9 %copy-done.2 = f32[1,192,128]{2,1,0:T(8,128)S(1)} copy-done((f32[1,192,128]{2,1,0:T(8,128)S(1)}, f32[1,192,128]{2,1,0:T(8,128)}, u32[]{:S(2)}) %copy-start.2) | copy-done | bytes 98328
  45.1 0.0 copy-start.3
  45.1 0.8 %copy-done.3 = bf16[2,128,128]{2,1,0:T(8,128)(2,1)S(1)} copy-done((bf16[2,128,128]{2,1,0:T(8,128)(2,1)S(1)}, bf16[2,128,128]{2,1,0:T(8,128)(2,1)}, u32[]{:S(2)}) %copy-start.3) | copy-done | bytes 65560
  45.9 2.0 %combine.1 = (bf16[128,4096]{1,0:T(8,128)(2,1)}, f32[1,192,768]{2,1,0:T(8,128)}, f32[1,192,128]{2,1,0:T(8,128)}) custom-call(bf16[4,128,1024]{2,1,0:T(8,128)(2,1)S(1)} %copy-done, bf16[2,128,128]{2,1,0:T(8,128)(2,1)S(1)} %copy-done.3, f32[1,192,768]{2,1,0:T(8,128)S(1)} %copy-done.1, f32[1,192,128]{2,1,0:T(8,128)S(1)} %copy-done.2), custom_call_target="tpu_custom_call" | custom-call | flops 268435456 | bytes 3473408 | tf_op jit(solution)/shard_map/combine/pallas_call | solution.py:468
Async XLA Ops:
  41.9 1.2 %copy-start = (bf16[4,128,1024]{2,1,0:T(8,128)(2,1)S(1)}, bf16[4,128,1024]{2,1,0:T(8,128)(2,1)}, u32[]{:S(2)}) copy-start(bf16[4,128,1024]{2,1,0:T(8,128)(2,1)} %get-tuple-element.7.returned) | copy-start | bytes 3145732
  43.1 1.1 %copy-start.1 = (f32[1,192,768]{2,1,0:T(8,128)S(1)}, f32[1,192,768]{2,1,0:T(8,128)}, u32[]{:S(2)}) copy-start(f32[1,192,768]{2,1,0:T(8,128)} %get-tuple-element.9.hessian_hbm) | copy-start | bytes 1769476
  44.2 0.9 %copy-start.2 = (f32[1,192,128]{2,1,0:T(8,128)S(1)}, f32[1,192,128]{2,1,0:T(8,128)}, u32[]{:S(2)}) copy-start(f32[1,192,128]{2,1,0:T(8,128)} %get-tuple-element.10.panel_hbm) | copy-start | bytes 294916
  45.1 0.8 %copy-start.3 = (bf16[2,128,128]{2,1,0:T(8,128)(2,1)S(1)}, bf16[2,128,128]{2,1,0:T(8,128)(2,1)}, u32[]{:S(2)}) copy-start(bf16[2,128,128]{2,1,0:T(8,128)(2,1)} %get-tuple-element.8.mix_ref) | copy-start | bytes 196612

commit v4 on v2

--- a/solution.py
+++ b/solution.py
@@ -12,6 +12,7 @@
 PANEL = 128
 CAP = 16
 CHUNKS = 4
+GROUP = 4
 MESH = pl.DeviceIdType.MESH
 HIGHEST = lax.Precision.HIGHEST
 
@@ -265,57 +266,79 @@
     row_number = lax.broadcasted_iota(jnp.int32, (PANEL, 1), 0)
     lane_number = lax.broadcasted_iota(jnp.int32, (1, PANEL), 1)
 
-    def eliminate(pair, carry):
-        j = 2 * pair
+    def eliminate(number, carry):
+        j = GROUP * number
+        group = range(GROUP)
         rest = elim[...]
-        row0 = elim[pl.ds(j, 1), :]
-        row1 = elim[pl.ds(j + 1, 1), :]
-        lane0 = lane_number == j
-        lane1 = lane_number == j + 1
-        pivot0 = jnp.sum(jnp.where(lane0, row0, 0.0), axis=1, keepdims=True)
-        cross = jnp.sum(jnp.where(lane1, row0, 0.0), axis=1, keepdims=True)
-        pivot1 = jnp.sum(jnp.where(lane1, row1, 0.0), axis=1, keepdims=True)
-        column0 = jnp.sum(jnp.where(lane0, rest, 0.0), axis=1, keepdims=True)
-        column1 = jnp.sum(jnp.where(lane1, rest, 0.0), axis=1, keepdims=True)
-        below = row_number > j + 1
-        scale0 = 1.0 / pivot0
-        ratio = cross * scale0
-        pivot1 = pivot1 - ratio * cross
-        scale1 = 1.0 / pivot1
-        factor0 = jnp.where(below, column0 * scale0, 0.0)
-        factor1 = jnp.where(below, (column1 - factor0 * cross) * scale1, 0.0)
-        next1 = jnp.where(lane0, -ratio, row1 - ratio * row0)
-        take0 = jnp.where(lane0, 1.0, jnp.where(lane1, 0.0, row0))
-        take1 = jnp.where(lane1, 1.0, next1)
-        cleared = jnp.logical_and(jnp.logical_or(lane0, lane1), below)
-        elim[...] = jnp.where(cleared, 0.0, rest) - factor0 * take0 - factor1 * take1
-        elim[pl.ds(j + 1, 1), :] = jnp.where(lane1, pivot1, next1)
+        rows = [elim[pl.ds(j + m, 1), :] for m in group]
+        lanes = [lane_number == j + m for m in group]
+        below = row_number > j + GROUP - 1
+
+        def pick(values, m):
+            return jnp.sum(jnp.where(lanes[m], values, 0.0), axis=1, keepdims=True)
+
+        cross = {(m, k): pick(rows[m], k) for m in group for k in range(m, GROUP)}
+        columns = [jnp.where(below, pick(rest, m), 0.0) for m in group]
+        factors = []
+        for m in group:
+            scale = 1.0 / cross[m, m]
+            factors.append(columns[m] * scale)
+            for k in range(m + 1, GROUP):
+                ratio = cross[m, k] * scale
+                columns[k] = columns[k] - factors[m] * cross[m, k]
+                rows[k] = jnp.where(lanes[m], -ratio, rows[k] - ratio * rows[m])
+                for q in range(k, GROUP):
+                    cross[k, q] = cross[k, q] - ratio * cross[m, q]
+        inside = jnp.logical_and(lane_number >= j, lane_number < j + GROUP)
+        updated = jnp.where(jnp.logical_and(inside, below), 0.0, rest)
+        for m in group:
+            later = jnp.logical_and(inside, lane_number > j + m)
+            taken = jnp.where(lanes[m], 1.0, jnp.where(later, 0.0, rows[m]))
+            updated = updated - factors[m] * taken
+        elim[...] = updated
+        for m in range(1, GROUP):
+            elim[pl.ds(j + m, 1), :] = rows[m]
         return carry
 
+    start, offset = window_of(place, share)
+
+    def partial(number):
+        rows = pl.ds(pl.multiple_of(number * slots, CAP), slots)
+        product = lax.dot_general(
+            hidden_all[rows, pl.ds(pl.multiple_of(start, 128), window)],
+            hidden_all[rows, :],
+            (((0,), (0,)), ((), ())),
+            preferred_element_type=jnp.float32,
+        )
+        return product * hess_scale
+
+    def add_received(step):
+        @pl.when(place >= step)
+        def _():
+            hess_buf[...] += partial(place - step)
+
+        @pl.when(place < pair_count - step)
+        def _():
+            hess_buf[...] += partial(place + step)
+
+    hess_buf[...] = partial(place)
+    groups = PANEL // GROUP
     first = 0
     for step in range(1, pair_count):
-        last = PANEL // 2 if step == pair_count - 1 else min(PANEL // 2, 28 * step - 12)
+        last = groups if step == pair_count - 1 else min(groups, 14 * step - 8)
         lax.fori_loop(first, last, eliminate, 0)
         first = last
         if step < pair_count - 1:
             receive(step)
             each_send(step + 1, lambda copy: copy.start())
+            add_received(step)
     done = elim[...]
     pivots = jnp.sum(jnp.where(diagonal, done, 0.0), axis=1, keepdims=True)
     inverse = jnp.where(row_ids > column_ids, done, jnp.where(diagonal, 1.0, 0.0))
     inverse = inverse * lax.rsqrt(pivots)
 
     receive(pair_count - 1)
-    start, offset = window_of(place, share)
-    hess_buf[...] = (
-        lax.dot_general(
-            hidden_all[:, pl.ds(pl.multiple_of(start, 128), window)],
-            hidden_all[...],
-            (((0,), (0,)), ((), ())),
-            preferred_element_type=jnp.float32,
-        )
-        * hess_scale
-    )
+    add_received(pair_count - 1)
     my_rows = pl.ds(pl.multiple_of(offset, 8), share)
     store_hessian = pltpu.make_async_copy(
         hess_buf.at[my_rows, :], hessian_hbm.at[0], store_sem.at[CHUNKS]

time: 46.2 us -> 46 us (level)
  no operation moved by 1% of the time
where the time goes in v4:
time: 46 us; the launch traced here: 45.8 us
  Pallas kernels  45.1 us (98%)
  between operations  0.64 us (1%)
    pallas_call x1, Pallas kernels, per_device(): pl.pallas_call(functools.partial(kernel, owners, pair_count, window), out...  41 us
    pallas_call x1, Pallas kernels, per_device(): pl.pallas_call(combine, grid=(CHUNKS,), out_shape=(jax.ShapeDtypeStruct((...  4.14 us

profile of v4, /device:TPU:0, one launch (start us, length us, event | category | flops | bytes accessed | tf_op | source)
XLA Modules:
  0.0 45.8 jit_solution(5790970825038061764)
XLA Ops:
  0.6 41.0 %experts.1 = (bf16[4,128,1024]{2,1,0:T(8,128)(2,1)}, bf16[2,128,128]{2,1,0:T(8,128)(2,1)}, f32[1,192,768]{2,1,0:T(8,128)}, f32[1,192,128]{2,1,0:T(8,128)}) custom-call(bf16[128,4096]{1,0:T(8,128)(2,1)} %tokens_ref.1, s32[8,128]{1,0:T(8,128)} %bitcast.2, f32[8,128]{1,0:T(8,128)} %bitcast.3, bf16[1,4096,768]{2,1,0:T(8,128)(2,1)} %gate_hbm.1, ...), custom_call_target="tpu_custom_call" | custom-call | flops 2415919104 | bytes 18874368 | tf_op jit(solution)/shard_map/experts/pallas_call | solution.py:401
  41.6 4.1 %combine.1 = (bf16[128,4096]{1,0:T(8,128)(2,1)}, f32[1,192,768]{2,1,0:T(8,128)}, f32[1,192,128]{2,1,0:T(8,128)}) custom-call(bf16[4,128,1024]{2,1,0:T(8,128)(2,1)} %get-tuple-element.7.returned_ref, bf16[2,128,128]{2,1,0:T(8,128)(2,1)} %get-tuple-element.8.mix_ref, f32[1,192,768]{2,1,0:T(8,128)} %get-tuple-element.9.hessian_ref, ...), custom_call_target="tpu_custom_call" | custom-call | flops 268435456 | bytes 3473408 | tf_op jit(solution)/shard_map/combine/pallas_call | solution.py:450

commit v5 on v4

--- a/solution.py
+++ b/solution.py
@@ -12,6 +12,7 @@
 PANEL = 128
 CAP = 16
 CHUNKS = 4
+STEPS = 2
 GROUP = 4
 MESH = pl.DeviceIdType.MESH
 HIGHEST = lax.Precision.HIGHEST
@@ -376,11 +377,13 @@
 
 
 def combine(returned_ref, mix_ref, hessian_ref, panel_ref, combined_ref, hessian_out, panel_out):
-    rows = returned_ref[0]
-    combined_ref[...] = (
-        jnp.dot(mix_ref[0], rows, preferred_element_type=jnp.float32)
-        + jnp.dot(mix_ref[1], rows, preferred_element_type=jnp.float32)
-    ).astype(jnp.bfloat16)
+    width = returned_ref.shape[2]
+    for c in range(returned_ref.shape[0]):
+        rows = returned_ref[c]
+        combined_ref[:, c * width : (c + 1) * width] = (
+            jnp.dot(mix_ref[0], rows, preferred_element_type=jnp.float32)
+            + jnp.dot(mix_ref[1], rows, preferred_element_type=jnp.float32)
+        ).astype(jnp.bfloat16)
     hessian_out[...] = hessian_ref[...]
     panel_out[...] = panel_ref[...]
 
@@ -444,25 +447,26 @@
         ),
         name="experts",
     )(tokens, expert_ids.T, route_weight.T, gate_weight, up_weight, down_weight)
-    strip = share // CHUNKS
+    strip = share // STEPS
+    per_step = CHUNKS // STEPS
     hessian_spec = pl.BlockSpec((1, strip, FF), lambda c: (0, c, 0))
     panel_spec = pl.BlockSpec((1, strip, PANEL), lambda c: (0, c, 0))
     return pl.pallas_call(
         combine,
-        grid=(CHUNKS,),
+        grid=(STEPS,),
         out_shape=(
             jax.ShapeDtypeStruct((tok_count, model_width), bf16),
             jax.ShapeDtypeStruct((1, share, FF), f32),
             jax.ShapeDtypeStruct((1, share, PANEL), f32),
         ),
         in_specs=[
-            pl.BlockSpec((1, slots, width), lambda c: (c, 0, 0)),
+            pl.BlockSpec((per_step, slots, width), lambda c: (c, 0, 0)),
             pl.BlockSpec((2, tok_count, slots), lambda c: (0, 0, 0)),
             hessian_spec,
             panel_spec,
         ],
         out_specs=(
-            pl.BlockSpec((tok_count, width), lambda c: (0, c)),
+            pl.BlockSpec((tok_count, per_step * width), lambda c: (0, c)),
             hessian_spec,
             panel_spec,
         ),

time: 46 us -> 44.7 us (0.972)
  Pallas kernels: 45.1 us -> 43.9 us
    pallas_call x1, Pallas kernels: 4.14 us -> 2.94 us  [per_device(): pl.pallas_call(combine, grid=(STEPS,), out_shape=(jax.ShapeDtypeStruct((t...]
where the time goes in v5:
time: 44.7 us; the launch traced here: 44.6 us
  Pallas kernels  43.9 us (98%)
  between operations  0.64 us (1%)
    pallas_call x1, Pallas kernels, per_device(): pl.pallas_call(functools.partial(kernel, owners, pair_count, window), out...  41 us
    pallas_call x1, Pallas kernels, per_device(): pl.pallas_call(combine, grid=(STEPS,), out_shape=(jax.ShapeDtypeStruct((t...  2.94 us

profile of v5, /device:TPU:0, one launch (start us, length us, event | category | flops | bytes accessed | tf_op | source)
XLA Modules:
  0.0 44.6 jit_solution(15687995350256592831)
XLA Ops:
  0.6 41.0 %experts.1 = (bf16[4,128,1024]{2,1,0:T(8,128)(2,1)}, bf16[2,128,128]{2,1,0:T(8,128)(2,1)}, f32[1,192,768]{2,1,0:T(8,128)}, f32[1,192,128]{2,1,0:T(8,128)}) custom-call(bf16[128,4096]{1,0:T(8,128)(2,1)} %tokens_ref.1, s32[8,128]{1,0:T(8,128)} %bitcast.2, f32[8,128]{1,0:T(8,128)} %bitcast.3, bf16[1,4096,768]{2,1,0:T(8,128)(2,1)} %gate_hbm.1, ...), custom_call_target="tpu_custom_call" | custom-call | flops 2415919104 | bytes 18874368 | tf_op jit(solution)/shard_map/experts/pallas_call | solution.py:404
  41.6 2.9 %combine.1 = (bf16[128,4096]{1,0:T(8,128)(2,1)}, f32[1,192,768]{2,1,0:T(8,128)}, f32[1,192,128]{2,1,0:T(8,128)}) custom-call(bf16[4,128,1024]{2,1,0:T(8,128)(2,1)} %get-tuple-element.7.returned_ref, bf16[2,128,128]{2,1,0:T(8,128)(2,1)} %get-tuple-element.8.mix_ref, f32[1,192,768]{2,1,0:T(8,128)} %get-tuple-element.9.hessian_ref, ...), custom_call_target="tpu_custom_call" | custom-call | flops 268435456 | bytes 3473408 | tf_op jit(solution)/shard_map/combine/pallas_call | solution.py:454
